TPU v7x, 128 devices: a whole 4x4x4 slice. The times are simulated.
128 devices in a mesh: rows: 16 (over y, z), cols: 8 (over x, core).
Axes of the slice: x: 4, y: 4, z: 4, core: 2. Of those that a mesh axis runs over, the one named last changes fastest.
Arguments:
- series: float32 [300, 32768], P(None, ('rows', 'cols')), may hold values from -6 to 6
- point_order: int32 [32768], P('rows'), may hold values from 0 to 32767, as said below
- step_block: int32 [8], replicated, may hold values from 16 to 31, as said below
- panel: float32 [32768, 8192], P('rows', 'cols'), may hold values from -0.09375 to 0.09375
- diag_inverse: float32 [32768, 1024], P('rows'), may hold values from -0.09375 to 1.09375
Outputs:
- solved: float32 [8192, 300], P(('rows', 'cols'))
- residual: float32 [32768, 300], P(('rows', 'cols'))
Inputs may be any that keep to these rules, and one draw needn't show every extreme that they name: Within each group of 2048 consecutive points, point_order is a permutation of the same group's indices. `step_block`: step k lies in block rows k * 2 + c to k * 2 + c + 1, with c = 16; the first step takes the first row of its range and the last step the last row of its range.
All inputs are finite; a program needn't handle non-finite values.
Results may differ from a plain program's by a relative error of at most 0.00014.
Values sent between devices are 32-bit elements; how exact they have to be, the bound alone decides.
A program may use at most 128 MiB of HBM per device.

v0:
```python
import jax
import jax.numpy as jnp
from jax import lax
from jax.sharding import PartitionSpec as P

STEPS = 8


def from_root(value, axis, source):
    kept = jnp.where(lax.axis_index(axis) == source, value, 0).astype(value.dtype)
    return lax.psum(kept, axis)


def body(series, point_order, step_block, panel, diag_inverse):
    highest = lax.Precision.HIGHEST
    gathered = lax.all_gather(series, "cols", axis=1, tiled=True)
    group_rows = gathered.shape[1]
    date_count = gathered.shape[0]
    block_size = diag_inverse.shape[1]
    local_blocks = group_rows // block_size
    per_column = panel.shape[1] // block_size
    local_index = point_order % group_rows
    right_side = jnp.take(gathered, local_index, axis=1).T
    column_index = lax.axis_index("cols")
    row_index = lax.axis_index("rows")
    flat_index = row_index * lax.axis_size("cols") + column_index
    out_rows = STEPS * block_size // (lax.axis_size("rows") * lax.axis_size("cols"))
    out_first = flat_index * out_rows
    target_section = out_first // block_size
    target_offset = out_first % block_size

    def product_rows(solution):
        return jnp.dot(panel, solution, precision=highest, preferred_element_type=jnp.float32)

    running = jnp.zeros((group_rows, date_count), jnp.float32)
    kept = jnp.zeros((out_rows, date_count), jnp.float32)
    for section in range(STEPS):
        slot_start = step_block[section] % local_blocks * block_size
        owner = step_block[section] // local_blocks
        partial_value = lax.dynamic_slice(
            running, (slot_start, jnp.int32(0)), (block_size, date_count)
        )
        summed = lax.psum(partial_value, "cols")
        pivot = (
            lax.dynamic_slice(right_side, (slot_start, jnp.int32(0)), (block_size, date_count))
            - summed
        )
        inverse = lax.dynamic_slice(
            diag_inverse, (slot_start, jnp.int32(0)), (block_size, block_size)
        )
        local_solution = jnp.dot(
            inverse, pivot, precision=highest, preferred_element_type=jnp.float32
        )
        solution = from_root(local_solution, "rows", owner)
        piece = lax.dynamic_slice(solution, (target_offset, jnp.int32(0)), (out_rows, date_count))
        kept = jnp.where(target_section == section, piece, kept)
        owned = section // per_column == column_index
        running = lax.cond(
            owned, lambda acc: acc + product_rows(solution), lambda acc: acc, running
        )
    share = lax.psum_scatter(running, "cols", scatter_dimension=0, tiled=True)
    share_rows = share.shape[0]
    own_side = lax.dynamic_slice(
        right_side, (column_index * share_rows, jnp.int32(0)), (share_rows, date_count)
    )
    return (kept, own_side - share)


def solution(mesh):
    in_specs = (P(None, ("rows", "cols")), P("rows"), P(), P("rows", "cols"), P("rows", None))
    out_specs = (P(("rows", "cols"), None), P(("rows", "cols"), None))
    return jax.shard_map(body, mesh=mesh, in_specs=in_specs, out_specs=out_specs, check_vma=False)
```

profile of v0, /device:TPU:45, one launch (start us, length us, event | category | flops | bytes accessed | tf_op | source)
XLA Modules:
  0.0 1407.2 jit_solution(2406514425381497610)
XLA Ops:
  14.8 23.7 %all-gather.2.cloned.1.call-done = f32[300,2048]{0,1:T(8,128)} async-done(((f32[300,256]{0,1:T(8,128)}), f32[300,2048]{0,1:T(8,128)}) %all-gather.2.cloned.1.call-update) | async-done | bytes 2457616 | tf_op jit(solution)/shard_map/all_gather | solution.py:16
  38.5 10.9 gather_fusion
  62.7 83.6 %all-reduce.16.cloned.1.call-done = f32[1024,300]{0,1:T(8,128)} async-done(((f32[1024,300]{0,1:T(8,128)}), f32[1024,300]{0,1:T(8,128)}) %all-reduce.16.cloned.1.call-update) | async-done | bytes 1228816 | tf_op jit(solution)/shard_map/psum | solution.py:11
  151.6 70.8 %all-reduce.18.cloned.1.call-done = f32[1024,300]{1,0:T(8,128)} async-done(((f32[1024,300]{1,0:T(8,128)}), f32[1024,300]{1,0:T(8,128)}) %all-reduce.18.cloned.1.call-update) | async-done | bytes 1228816 | tf_op jit(solution)/shard_map/psum | solution.py:43
  233.1 85.2 %all-reduce.20.cloned.1.call-done = f32[1024,300]{0,1:T(8,128)} async-done(((f32[1024,300]{0,1:T(8,128)}), f32[1024,300]{0,1:T(8,128)}) %all-reduce.20.cloned.1.call-update) | async-done | bytes 1228816 | tf_op jit(solution)/shard_map/psum | solution.py:11
  323.4 68.9 %all-reduce.22.cloned.1.call-done = f32[1024,300]{1,0:T(8,128)} async-done(((f32[1024,300]{1,0:T(8,128)}), f32[1024,300]{1,0:T(8,128)}) %all-reduce.22.cloned.1.call-update) | async-done | bytes 1228816 | tf_op jit(solution)/shard_map/psum | solution.py:43
  392.3 8.5 fusion.23
  402.8 85.4 %all-reduce.24.cloned.1.call-done = f32[1024,300]{0,1:T(8,128)} async-done(((f32[1024,300]{0,1:T(8,128)}), f32[1024,300]{0,1:T(8,128)}) %all-reduce.24.cloned.1.call-update) | async-done | bytes 1228816 | tf_op jit(solution)/shard_map/psum | solution.py:11
  493.5 71.8 %all-reduce.26.cloned.1.call-done = f32[1024,300]{1,0:T(8,128)} async-done(((f32[1024,300]{1,0:T(8,128)}), f32[1024,300]{1,0:T(8,128)}) %all-reduce.26.cloned.1.call-update) | async-done | bytes 1228816 | tf_op jit(solution)/shard_map/psum | solution.py:43
  565.3 8.5 fusion.26
  575.8 85.3 %all-reduce.28.cloned.1.call-done = f32[1024,300]{0,1:T(8,128)} async-done(((f32[1024,300]{0,1:T(8,128)}), f32[1024,300]{0,1:T(8,128)}) %all-reduce.28.cloned.1.call-update) | async-done | bytes 1228816 | tf_op jit(solution)/shard_map/psum | solution.py:11
  666.2 69.9 %all-reduce.30.cloned.1.call-done = f32[1024,300]{1,0:T(8,128)} async-done(((f32[1024,300]{1,0:T(8,128)}), f32[1024,300]{1,0:T(8,128)}) %all-reduce.30.cloned.1.call-update) | async-done | bytes 1228816 | tf_op jit(solution)/shard_map/psum | solution.py:43
  736.1 8.5 fusion.29
  746.8 85.2 %all-reduce.32.cloned.1.call-done = f32[1024,300]{0,1:T(8,128)} async-done(((f32[1024,300]{0,1:T(8,128)}), f32[1024,300]{0,1:T(8,128)}) %all-reduce.32.cloned.1.call-update) | async-done | bytes 1228816 | tf_op jit(solution)/shard_map/psum | solution.py:11
  837.1 73.5 %all-reduce.34.cloned.1.call-done = f32[1024,300]{1,0:T(8,128)} async-done(((f32[1024,300]{1,0:T(8,128)}), f32[1024,300]{1,0:T(8,128)}) %all-reduce.34.cloned.1.call-update) | async-done | bytes 1228816 | tf_op jit(solution)/shard_map/psum | solution.py:43
  921.2 85.2 %all-reduce.36.cloned.1.call-done = f32[1024,300]{0,1:T(8,128)} async-done(((f32[1024,300]{0,1:T(8,128)}), f32[1024,300]{0,1:T(8,128)}) %all-reduce.36.cloned.1.call-update) | async-done | bytes 1228816 | tf_op jit(solution)/shard_map/psum | solution.py:11
  1006.5 11.2 conditional.13
  1006.5 11.2 convolution_add_fusion.4
  1023.0 59.8 %all-reduce.38.cloned.1.call-done = f32[1024,300]{1,0:T(8,128)} async-done(((f32[1024,300]{1,0:T(8,128)}), f32[1024,300]{1,0:T(8,128)}) %all-reduce.38.cloned.1.call-update) | async-done | bytes 1228816 | tf_op jit(solution)/shard_map/psum | solution.py:43
  1093.4 85.3 %all-reduce.40.cloned.1.call-done = f32[1024,300]{0,1:T(8,128)} async-done(((f32[1024,300]{0,1:T(8,128)}), f32[1024,300]{0,1:T(8,128)}) %all-reduce.40.cloned.1.call-update) | async-done | bytes 1228816 | tf_op jit(solution)/shard_map/psum | solution.py:11
  1183.8 73.3 %all-reduce.42.cloned.1.call-done = f32[1024,300]{1,0:T(8,128)} async-done(((f32[1024,300]{1,0:T(8,128)}), f32[1024,300]{1,0:T(8,128)}) %all-reduce.42.cloned.1.call-update) | async-done | bytes 1228816 | tf_op jit(solution)/shard_map/psum | solution.py:43
  1257.1 8.5 fusion.17
  1265.7 87.3 %all-reduce.44.cloned.1.call-done = f32[1024,300]{0,1:T(8,128)} async-done(((f32[1024,300]{0,1:T(8,128)}), f32[1024,300]{0,1:T(8,128)}) %all-reduce.44.cloned.1.call-update) | async-done | bytes 1228816 | tf_op jit(solution)/shard_map/psum | solution.py:11
  1357.9 40.6 %reduce-scatter.2.cloned.1.call-done = f32[256,300]{1,0:T(8,128)} async-done(((f32[2048,300]{1,0:T(8,128)}), f32[256,300]{1,0:T(8,128)}) %reduce-scatter.2.cloned.1.call-update) | async-done | bytes 307216 | tf_op jit(solution)/shard_map/reduce_scatter | solution.py:61
  (72 shorter events, 81.0 us)
Async XLA Ops:
  7.2 31.3 %all-gather.2.cloned.1.call-start = ((), (), s32[]{:S(2)}) async-start(), calls=%async_computation.1 | async-start | bytes 3538944 | tf_op jit(solution)/shard_map/all_gather | solution.py:16
  9.1 137.2 %all-reduce.16.cloned.1.call-start = ((), (), s32[]{:S(2)}) async-start(), calls=%async_computation.2 | async-start | bytes 2490368 | tf_op jit(solution)/shard_map/psum | solution.py:11
  51.5 1.7 copy-start
  60.9 161.5 %all-reduce.18.cloned.1.call-start = ((), (), s32[]{:S(2)}) async-start(), calls=%async_computation.3 | async-start | bytes 3145728 | tf_op jit(solution)/shard_map/psum | solution.py:43
  150.8 167.5 %all-reduce.20.cloned.1.call-start = ((), (), s32[]{:S(2)}) async-start(), calls=%async_computation.4 | async-start | bytes 2490368 | tf_op jit(solution)/shard_map/psum | solution.py:11
  231.0 161.4 %all-reduce.22.cloned.1.call-start = ((), (), s32[]{:S(2)}) async-start(), calls=%async_computation.5 | async-start | bytes 3145728 | tf_op jit(solution)/shard_map/psum | solution.py:43
  322.5 165.8 %all-reduce.24.cloned.1.call-start = ((), (), s32[]{:S(2)}) async-start(), calls=%async_computation.6 | async-start | bytes 2490368 | tf_op jit(solution)/shard_map/psum | solution.py:11
  400.9 164.4 %all-reduce.26.cloned.1.call-start = ((), (), s32[]{:S(2)}) async-start(), calls=%async_computation.7 | async-start | bytes 3145728 | tf_op jit(solution)/shard_map/psum | solution.py:43
  492.4 168.8 %all-reduce.28.cloned.1.call-start = ((), (), s32[]{:S(2)}) async-start(), calls=%async_computation.8 | async-start | bytes 2490368 | tf_op jit(solution)/shard_map/psum | solution.py:11
  573.8 162.3 %all-reduce.30.cloned.1.call-start = ((), (), s32[]{:S(2)}) async-start(), calls=%async_computation.9 | async-start | bytes 3145728 | tf_op jit(solution)/shard_map/psum | solution.py:43
  665.3 166.7 %all-reduce.32.cloned.1.call-start = ((), (), s32[]{:S(2)}) async-start(), calls=%async_computation.10 | async-start | bytes 2490368 | tf_op jit(solution)/shard_map/psum | solution.py:11
  744.6 165.9 %all-reduce.34.cloned.1.call-start = ((), (), s32[]{:S(2)}) async-start(), calls=%async_computation.11 | async-start | bytes 3145728 | tf_op jit(solution)/shard_map/psum | solution.py:43
  836.1 170.3 %all-reduce.36.cloned.1.call-start = ((), (), s32[]{:S(2)}) async-start(), calls=%async_computation.12 | async-start | bytes 2490368 | tf_op jit(solution)/shard_map/psum | solution.py:11
  919.1 163.8 %all-reduce.38.cloned.1.call-start = ((), (), s32[]{:S(2)}) async-start(), calls=%async_computation.13 | async-start | bytes 3145728 | tf_op jit(solution)/shard_map/psum | solution.py:43
  1021.9 156.9 %all-reduce.40.cloned.1.call-start = ((), (), s32[]{:S(2)}) async-start(), calls=%async_computation.14 | async-start | bytes 2490368 | tf_op jit(solution)/shard_map/psum | solution.py:11
  1091.4 165.7 %all-reduce.42.cloned.1.call-start = ((), (), s32[]{:S(2)}) async-start(), calls=%async_computation.15 | async-start | bytes 3145728 | tf_op jit(solution)/shard_map/psum | solution.py:43
  1182.9 170.1 %all-reduce.44.cloned.1.call-start = ((), (), s32[]{:S(2)}) async-start(), calls=%async_computation.16 | async-start | bytes 2490368 | tf_op jit(solution)/shard_map/psum | solution.py:11
  1265.6 132.9 %reduce-scatter.2.cloned.1.call-start = ((), (), s32[]{:S(2)}) async-start(), calls=%async_computation.17 | async-start | bytes 3538944 | tf_op jit(solution)/shard_map/reduce_scatter | solution.py:61
Sparse Core Ops, SparseCore 0:
  9.7 28.7 all-gather.1
  61.0 85.2 all-reduce.15
  150.9 71.5 all-reduce.17
  231.1 87.1 all-reduce.19
  322.6 69.7 all-reduce.21
  401.0 87.1 all-reduce.23
  492.5 72.7 all-reduce.25
  573.9 87.1 all-reduce.27
  665.4 70.6 all-reduce.29
  744.8 87.1 all-reduce.31
  836.3 74.2 all-reduce.33
  919.2 87.1 all-reduce.35
  1022.0 60.8 all-reduce.37
  1091.5 87.1 all-reduce.39
  1183.0 74.0 all-reduce.41
  1265.8 87.1 all-reduce.43
  1355.5 42.9 reduce-scatter.1
where the time goes:
time: 1420 us; the launch traced here: 1410 us
  waiting for transfers between devices  1240 us (87%)
  matrix products  78.5 us (6%)
  local copies, waits for them, and re-layouts  49.2 us (3%)
  between operations  35.3 us (2%)
    psum x8, waiting for transfers between devices, from_root(): return lax.psum(kept, axis)  683 us
    psum x7, waiting for transfers between devices, body(): summed = lax.psum(partial_value, 'cols')  488 us
    dot_general x8, matrix products, body(): jnp.dot(inverse, pivot, precision=highest, preferred_element_type=jnp.flo...  67.2 us
    reduce_scatter x1, waiting for transfers between devices, body(): share = lax.psum_scatter(running, 'cols', scatter_dimension=0, tiled=True)  40.6 us
  transfers between devices with their start and end apart: 17, of which 17 were waited for; matrix products, arithmetic and copies ran while one was open for 0% of the time, Pallas kernels for 0%

commit v1 on v0

v1 whole, which is shorter than its diff:
```python
import jax
import jax.numpy as jnp
from jax import lax
from jax.experimental import pallas as pl
from jax.experimental.pallas import tpu as pltpu
from jax.sharding import PartitionSpec as P

MESH = pl.DeviceIdType.MESH
F32 = jnp.float32
BF16 = jnp.bfloat16
CHUNKS = 5
CD = 64
BS = 1024
COLS = 8
PIECE = 256
FIRST = 8


def split2(v):
    hi = v.astype(BF16)
    return hi, (v - hi.astype(F32)).astype(BF16)


def split3(v):
    hi = v.astype(BF16)
    rest = v - hi.astype(F32)
    mid = rest.astype(BF16)
    return hi, mid, (rest - mid.astype(F32)).astype(BF16)


def nt(a, b):
    return lax.dot_general(a, b, (((1,), (1,)), ((), ())), preferred_element_type=F32)


def nn(a, b):
    return lax.dot_general(a, b, (((1,), (0,)), ((), ())), preferred_element_type=F32)


def kernel(step_ref, idx_ref, ser_ref, panel_ref, diag_ref, res_ref, sol_ref,
           pf, df, phi, plo, mhi, mlo, dhi, dlo, oh, ohr, gbuf, xbuf, pbuf, obuf, zbuf, rbuf, sbuf,
           pl_sem, dl_sem, gs_sem, gr_sem, f_sem, x_sem, o_sem, p_sem, zs_sem, zr_sem, ss_sem, sr_sem):
    r = lax.axis_index("rows")
    c = lax.axis_index("cols")
    k = r - FIRST
    y, z = r // 4, r % 4
    root = FIRST + 1 + jnp.minimum(c, 6)
    dy = (y - root // 4 + 4) % 4
    dz = (z - root % 4 + 4) % 4
    late = r >= FIRST
    chain = jnp.logical_and(late, c < k)
    starts = jnp.logical_and(late, c == 7)
    uses_d = jnp.logical_or(chain, starts)
    final_col = (k + 15) % 8
    final = jnp.logical_and(late, c == final_col)
    produces = uses_d
    diag_src = jnp.logical_and(final, r < 15)
    diag_dst = jnp.logical_and(c < 7, r == root)
    out_row = jnp.minimum(r + 1, 15)
    prev_col = (c + 7) % 8
    next_col = (c + 1) % 8

    zp, zm = y * 4 + (z + 1) % 4, y * 4 + (z + 3) % 4
    yp, ym = ((y + 1) % 4) * 4 + z, ((y + 3) % 4) * 4 + z

    barrier = pltpu.get_barrier_semaphore()
    for other in (zp, zm, yp, ym):
        pl.semaphore_signal(barrier, inc=1, device_id=(other, c), device_id_type=MESH)
    for d in range(1, COLS):
        pl.semaphore_signal(barrier, inc=1, device_id=(r, (c + d) % COLS), device_id_type=MESH)

    @pl.when(diag_src)
    def _():
        pl.semaphore_signal(barrier, inc=1, device_id=(out_row, k), device_id_type=MESH)

    @pl.when(diag_dst)
    def _():
        pl.semaphore_signal(barrier, inc=1, device_id=(r - 1, prev_col), device_id_type=MESH)

    def load_d(j):
        return pltpu.make_async_copy(diag_ref.at[pl.ds(j * PIECE, PIECE)], df.at[pl.ds(j * PIECE, PIECE)], dl_sem.at[j])

    def load_p(j):
        return pltpu.make_async_copy(panel_ref.at[pl.ds(j * PIECE, PIECE)], pf.at[pl.ds(j * PIECE, PIECE)], pl_sem.at[j])

    @pl.when(uses_d)
    def _():
        for j in range(8):
            load_d(j).start()

    for j in range(8):
        load_p(j).start()

    pl.semaphore_wait(barrier, 11 + diag_src.astype(jnp.int32) + diag_dst.astype(jnp.int32))

    def g_copy(src, i):
        return pltpu.make_async_remote_copy(
            src_ref=ser_ref.at[i], dst_ref=gbuf.at[src, i], send_sem=gs_sem.at[i],
            recv_sem=gr_sem.at[src, i], device_id=(r, 7), device_id_type=MESH)

    def x_copy(e, i, row):
        return pltpu.make_async_remote_copy(
            src_ref=xbuf.at[i], dst_ref=xbuf.at[i], send_sem=f_sem.at[e, i],
            recv_sem=x_sem.at[i], device_id=(row, c), device_id_type=MESH)

    def out_copy(i):
        return pltpu.make_async_remote_copy(
            src_ref=obuf.at[i], dst_ref=xbuf.at[i], send_sem=o_sem.at[i],
            recv_sem=x_sem.at[i], device_id=(out_row, k), device_id_type=MESH)

    def part_copy(i):
        return pltpu.make_async_remote_copy(
            src_ref=obuf.at[i], dst_ref=pbuf.at[i], send_sem=o_sem.at[i],
            recv_sem=p_sem.at[i], device_id=(r, next_col), device_id_type=MESH)

    def z_copy(i, d):
        return pltpu.make_async_remote_copy(
            src_ref=zbuf.at[i, d], dst_ref=rbuf.at[c, i], send_sem=zs_sem.at[i, d],
            recv_sem=zr_sem.at[c, i], device_id=(r, d), device_id_type=MESH)

    def z_wait(src, i):
        pltpu.make_async_remote_copy(
            src_ref=zbuf.at[i, src], dst_ref=rbuf.at[src, i], send_sem=zs_sem.at[i, src],
            recv_sem=zr_sem.at[src, i], device_id=(r, src), device_id_type=MESH).wait_recv()

    solver_col = r // 2
    sol_src = c == solver_col

    def s_copy(i, d):
        lane = pl.multiple_of((r % 2) * 512 + (d // 2) * 128, 128)
        return pltpu.make_async_remote_copy(
            src_ref=xbuf.at[i, :, pl.ds(lane, 128)], dst_ref=sbuf.at[i], send_sem=ss_sem.at[i, d],
            recv_sem=sr_sem.at[i], device_id=(r, d), device_id_type=MESH)

    edges = (
        (jnp.logical_and(dy == 0, dz <= 1), zp),
        (jnp.logical_and(dy == 0, dz == 0), zm),
        (dy <= 1, yp),
        (dy == 0, ym),
    )

    def send_out(i):
        @pl.when(final)
        def _():
            out_copy(i).start()

        @pl.when(jnp.logical_not(final))
        def _():
            part_copy(i).start()

    @pl.when(jnp.logical_and(late, c < 7))
    def _():
        @pl.loop(0, CHUNKS)
        def _(i):
            g_copy(c, i).start()

    slot = step_ref[jnp.maximum(k, 0)] - 2 * r

    def pick(first, second):
        return jnp.where(jnp.full(first.shape, slot, jnp.int32) == 0, first, second)

    shift = r * (COLS * PIECE)

    @pl.when(uses_d)
    def _():
        @pl.loop(0, 8)
        def _(j):
            load_d(j).wait()

        @pl.loop(0, 8)
        def _(j):
            rows = pl.ds(pl.multiple_of(j * 128, 128), 128)
            hi, lo = split2(pick(df[rows, :], df[pl.ds(pl.multiple_of(BS + j * 128, 128), 128), :]))
            dhi[rows, :] = hi
            dlo[rows, :] = lo

    @pl.when(starts)
    def _():
        for q in range(4):
            want = pick(idx_ref[q:q + 1, :], idx_ref[4 + q:5 + q, :]) - shift

            @pl.loop(0, COLS)
            def _(s):
                pos = lax.broadcasted_iota(jnp.int32, (PIECE, PIECE), 0) + s * PIECE
                oh[pl.ds(pl.multiple_of(s * PIECE, PIECE), PIECE), q * PIECE:(q + 1) * PIECE] = (
                    jnp.where(pos == want, 1.0, 0.0).astype(BF16))

        @pl.loop(0, CHUNKS)
        def _(i):
            hi, lo = split2(ser_ref[i])
            acc = nn(jnp.concatenate([hi, lo], axis=0), oh[7 * PIECE:, :])
            for s in range(7):
                pltpu.make_async_remote_copy(
                    src_ref=ser_ref.at[i], dst_ref=gbuf.at[s, i], send_sem=gs_sem.at[i],
                    recv_sem=gr_sem.at[s, i], device_id=(r, s), device_id_type=MESH).wait_recv()
                hi, lo = split2(gbuf[s, i])
                acc = acc + nn(jnp.concatenate([hi, lo], axis=0), oh[s * PIECE:(s + 1) * PIECE, :])
            both = acc.astype(BF16)
            out = nt(both, dhi[...])
            obuf[i] = out[:CD] + out[CD:] + nt(both[:CD], dlo[...])
            send_out(i)

    @pl.loop(0, 8)
    def _(j):
        load_p(j).wait()
        rows = pl.ds(pl.multiple_of(j * PIECE, PIECE), PIECE)
        hi, lo = split2(pf[rows, :])
        phi[rows, :] = hi
        plo[rows, :] = lo

    @pl.when(chain)
    def _():
        @pl.loop(0, 8)
        def _(j):
            rows = pl.ds(pl.multiple_of(j * 128, 128), 128)
            other = pl.ds(pl.multiple_of(BS + j * 128, 128), 128)
            hi, lo = split2(pick(pf[rows, :], pf[other, :]))
            oh[rows, :] = hi
            oh[other, :] = lo

        @pl.loop(0, 4)
        def _(j):
            rows = pl.ds(pl.multiple_of(j * PIECE, PIECE), PIECE)
            th = dhi[rows, :]
            ph = oh[:BS, :]
            m = nn(th, ph) + nn(dlo[rows, :], ph) + nn(th, oh[BS:, :])
            hi, lo = split2(m)
            mhi[rows, :] = hi
            mlo[rows, :] = lo

    @pl.loop(0, COLS)
    def _(d):
        want = idx_ref[pl.ds(d, 1), :] - shift
        pos = lax.broadcasted_iota(jnp.int32, (PIECE, PIECE), 0) + c * PIECE
        ohr[d] = jnp.where(pos == want, 1.0, 0.0).astype(BF16)

    def residual(i):
        hi, lo = split2(xbuf[i])
        both = jnp.concatenate([hi, lo], axis=0)
        three = jnp.concatenate(split3(ser_ref[i]), axis=0)

        @pl.loop(0, COLS)
        def _(d):
            rows = pl.ds(pl.multiple_of(d * PIECE, PIECE), PIECE)
            a = nt(both, phi[rows, :])
            a = a[:CD] + a[CD:] + nt(hi, plo[rows, :])
            b = nn(three, ohr[d])
            b = b[:CD] + (b[CD:2 * CD] + b[2 * CD:])

            @pl.when(d == c)
            def _():
                rbuf[c, i] = b - a

            @pl.when(d != c)
            def _():
                zbuf[i, d] = b - a
                z_copy(i, d).start()

    @pl.loop(0, CHUNKS)
    def _(i):
        x_copy(0, i, zp).wait_recv()
        for e, (cond, row) in enumerate(edges):
            @pl.when(cond)
            def _():
                x_copy(e, i, row).start()

        @pl.when(chain)
        def _():
            hi, lo = split2(xbuf[i])
            a = nt(jnp.concatenate([hi, lo], axis=0), mhi[...])
            a = a[:CD] + a[CD:] + nt(hi, mlo[...])
            part_copy(i).wait_recv()
            obuf[i] = pbuf[i] - a
            send_out(i)

        @pl.when(sol_src)
        def _():
            for d in range(COLS):
                @pl.when(d != c)
                def _():
                    s_copy(i, d).start()
            lane = pl.multiple_of((r % 2) * 512 + (c // 2) * 128, 128)
            sol_ref[i] = xbuf[i, :, pl.ds(lane, 128)]

        @pl.when(jnp.logical_not(chain))
        def _():
            residual(i)

    @pl.when(chain)
    def _():
        @pl.loop(0, CHUNKS)
        def _(i):
            residual(i)

    @pl.loop(0, CHUNKS)
    def _(i):
        @pl.when(jnp.logical_not(sol_src))
        def _():
            s_copy(i, c).wait_recv()
            sol_ref[i] = sbuf[i]

        @pl.loop(0, COLS)
        def _(s):
            @pl.when(s != c)
            def _():
                z_wait(s, i)

        acc = rbuf[0, i]
        for s in range(1, COLS):
            acc = acc + rbuf[s, i]
        res_ref[i] = acc

        @pl.when(jnp.logical_and(late, c < 7))
        def _():
            g_copy(c, i).wait_send()

        for e, (cond, row) in enumerate(edges):
            @pl.when(cond)
            def _():
                x_copy(e, i, row).wait_send()

        @pl.when(produces)
        def _():
            part_copy(i).wait_send()

        @pl.loop(0, COLS)
        def _(d):
            @pl.when(d != c)
            def _():
                z_copy(i, d).wait_send()

                @pl.when(sol_src)
                def _():
                    s_copy(i, d).wait_send()


def body(series, point_order, step_block, panel, diag_inverse):
    dates = series.shape[0]
    ser = jnp.pad(series, ((0, CHUNKS * CD - dates), (0, 0))).reshape(CHUNKS, CD, PIECE)
    idx = point_order.reshape(COLS, PIECE)
    vmem = pl.BlockSpec(memory_space=pltpu.VMEM)
    hbm = pl.BlockSpec(memory_space=pl.ANY)
    dma = pltpu.SemaphoreType.DMA
    res, sol = pl.pallas_call(
        kernel,
        out_shape=(
            jax.ShapeDtypeStruct((CHUNKS, CD, PIECE), F32),
            jax.ShapeDtypeStruct((CHUNKS, CD, 128), F32),
        ),
        in_specs=[pl.BlockSpec(memory_space=pltpu.SMEM), vmem, vmem, hbm, hbm],
        out_specs=(vmem, vmem),
        scratch_shapes=[
            pltpu.VMEM((2 * BS, BS), F32),
            pltpu.VMEM((2 * BS, BS), F32),
            pltpu.VMEM((2 * BS, BS), BF16),
            pltpu.VMEM((2 * BS, BS), BF16),
            pltpu.VMEM((BS, BS), BF16),
            pltpu.VMEM((BS, BS), BF16),
            pltpu.VMEM((BS, BS), BF16),
            pltpu.VMEM((BS, BS), BF16),
            pltpu.VMEM((2 * BS, BS), BF16),
            pltpu.VMEM((COLS, PIECE, PIECE), BF16),
            pltpu.VMEM((7, CHUNKS, CD, PIECE), F32),
            pltpu.VMEM((CHUNKS, CD, BS), F32),
            pltpu.VMEM((CHUNKS, CD, BS), F32),
            pltpu.VMEM((CHUNKS, CD, BS), F32),
            pltpu.VMEM((CHUNKS, COLS, CD, PIECE), F32),
            pltpu.VMEM((COLS, CHUNKS, CD, PIECE), F32),
            pltpu.VMEM((CHUNKS, CD, 128), F32),
            dma((8,)),
            dma((8,)),
            dma((CHUNKS,)),
            dma((7, CHUNKS)),
            dma((4, CHUNKS)),
            dma((CHUNKS,)),
            dma((CHUNKS,)),
            dma((CHUNKS,)),
            dma((CHUNKS, COLS)),
            dma((COLS, CHUNKS)),
            dma((CHUNKS, COLS)),
            dma((CHUNKS,)),
        ],
        compiler_params=pltpu.CompilerParams(
            collective_id=0, has_side_effects=True, vmem_limit_bytes=60 * 1024 * 1024
        ),
    )(step_block, idx, ser, panel, diag_inverse)
    residual = res.reshape(CHUNKS * CD, PIECE)[:dates].T
    half = lax.dynamic_slice_in_dim(sol, lax.axis_index("cols") % 2 * 64, 64, 2)
    solved = half.reshape(CHUNKS * CD, 64)[:dates].T
    return solved, residual


def solution(mesh):
    in_specs = (P(None, ("rows", "cols")), P("rows"), P(), P("rows", "cols"), P("rows", None))
    out_specs = (P(("rows", "cols"), None), P(("rows", "cols"), None))
    return jax.shard_map(body, mesh=mesh, in_specs=in_specs, out_specs=out_specs, check_vma=False)
```

time: 1420 us -> 156 us (0.11)
  waiting for transfers between devices: 1240 us -> 0 us
  Pallas kernels: 0 us -> 148 us
  matrix products: 78.5 us -> 0 us
  local copies, waits for them, and re-layouts: 49.2 us -> 6.49 us
  between operations: 35.3 us -> 0.67 us
    psum x15 -> x0, waiting for transfers between devices: 1170 us -> none  [the longest x8 683 us: from_root(): return lax.psum(kept, axis)]
    pallas_call x0 -> x1, Pallas kernels: none -> 148 us  [body(): pl.pallas_call(kernel, out_shape=(jax.ShapeDtypeStruct((CHUNKS, CD, PIECE...]
    dot_general x9 -> x0, matrix products: 78.5 us -> none  [the longest x8 67.2 us: body(): jnp.dot(inverse, pivot, precision=highest, preferred_element_type=jnp.flo...]
    reduce_scatter x1 -> x0, waiting for transfers between devices: 40.6 us -> none  [body(): share = lax.psum_scatter(running, 'cols', scatter_dimension=0, tiled=True)]
    unnamed x12 -> x1, local copies, waits for them, and re-layouts: 25.9 us -> 0.76 us
    all_gather x1 -> x0, waiting for transfers between devices: 23.7 us -> none  [body(): gathered = lax.all_gather(series, 'cols', axis=1, tiled=True)]
  transfers between devices with their start and end apart: 17 -> 0, of which waited for: 17 -> 0; matrix products, arithmetic and copies ran while one was open for 0% -> 0% of each run, Pallas kernels for 0% -> 0%
where the time goes in v1:
time: 156 us
  Pallas kernels  148 us (95%)
  local copies, waits for them, and re-layouts  6.49 us (4%)
    pallas_call x1, Pallas kernels, body(): pl.pallas_call(kernel, out_shape=(jax.ShapeDtypeStruct((CHUNKS, CD, PIECE...  148 us

profile of v1, /device:TPU:45, one launch (start us, length us, event | category | flops | bytes accessed | tf_op | source)
XLA Modules:
  0.0 155.6 jit_solution(5297529088780070355)
XLA Ops:
  0.6 1.3 reshape.16.idx_ref
  1.9 1.7 %pad.4 = f32[320,256]{1,0:T(8,128)} pad(f32[300,256]{1,0:T(8,128)} %param.5, f32[]{:T(128)} %constant.17.clone.1), padding=0_20x0_0 | pad | bytes 634884 | tf_op jit(solution)/shard_map/jit(_pad)/pad | solution.py:338
  3.6 148.4 %shard_map.68 = (f32[5,64,256]{2,1,0:T(8,128)}, f32[5,64,128]{2,1,0:T(8,128)}) custom-call(s32[8]{0:T(128)} %step_ref.1, s32[8,256]{1,0:T(8,128)} %reshape.16.idx_ref, f32[5,64,256]{2,1,0:T(8,128)} %bitcast.7, f32[2048,1024]{1,0:T(8,128)} %panel_ref.1, f32[2048,1024]{1,0:T(8,128)} %diag_ref.1), custom_call_target="tpu_custom_call" | custom-call | tf_op jit(solution)/shard_map/pallas_call | solution.py:343
  152.1 1.0 constant_dynamic-slice_fusion
  153.1 0.8 copy.7
  153.9 1.7 %slice_bitcast_fusion = f32[256,300]{0,1:T(8,128)} fusion(f32[320,256]{1,0:T(8,128)} %bitcast.9), kind=kLoop, calls=%fused_computation | loop fusion | bytes 614400 | tf_op jit(solution)/shard_map/transpose | solution.py:386
  (1 shorter events, 0.0 us)

commit v2 on v1

v2 whole, which is shorter than its diff:
```python
import jax
import jax.numpy as jnp
from jax import lax
from jax.experimental import pallas as pl
from jax.experimental.pallas import tpu as pltpu
from jax.sharding import PartitionSpec as P

MESH = pl.DeviceIdType.MESH
F32 = jnp.float32
BF16 = jnp.bfloat16
DATES = 300
CHUNKS = 10
CD = 32
PAIRS = CHUNKS // 2
PD = 2 * CD
ALL = CHUNKS * CD
BS = 1024
COLS = 8
CHIPS = 4
PIECE = 256
FIRST = 8


def split2(v):
    hi = v.astype(BF16)
    return hi, (v - hi.astype(F32)).astype(BF16)


def split3(v):
    hi = v.astype(BF16)
    rest = v - hi.astype(F32)
    mid = rest.astype(BF16)
    return hi, mid, (rest - mid.astype(F32)).astype(BF16)


def nn(a, b):
    return lax.dot_general(a, b, (((1,), (0,)), ((), ())), preferred_element_type=F32)


def times(hi, lo, weight_hi, weight_lo):
    n = hi.shape[0]
    a = nn(jnp.concatenate([hi, lo], axis=0), weight_hi)
    return a[:n] + (a[n:] + nn(hi, weight_lo))


def span(j, size):
    return pl.ds(pl.multiple_of(j * size, size), size)


def kernel(step_ref, idx_ref, ser_ref, panel_ref, diag_ref, res_ref, sol_ref,
           pf, df, phi, plo, mhi, mlo, dhi, dlo, oh, ohr, serp, gbuf, xbuf, pbuf, obuf, zbuf, zin, rbuf, sbuf,
           pl_sem, dl_sem, gs_sem, gr_sem, f_sem, x_sem, o_sem, p_sem, zs_sem, zr_sem, hs_sem, hr_sem, ss_sem, sr_sem):
    r = lax.axis_index("rows")
    c = lax.axis_index("cols")
    k = r - FIRST
    y, z = r // 4, r % 4
    chip, core = c // 2, c % 2
    root = FIRST + 1 + jnp.minimum(c, 6)
    dy = (y - root // 4 + 4) % 4
    dz = (z - root % 4 + 4) % 4
    late = r >= FIRST
    chain = jnp.logical_and(late, c < k)
    starts = jnp.logical_and(late, c == 7)
    gives = jnp.logical_and(late, c < 7)
    uses_d = jnp.logical_or(chain, starts)
    two = jnp.logical_and(chain, k == 1)
    bulk = jnp.logical_and(late, 2 * chip < k)
    final = jnp.logical_and(late, c == (k + 15) % 8)
    diag_src = jnp.logical_and(final, r < 15)
    diag_dst = jnp.logical_and(c < 7, r == root)
    out_row = jnp.minimum(r + 1, 15)
    prev_col = (c + 7) % 8
    next_col = (c + 1) % 8
    sol_src = c == r // 2

    zp, zm = y * 4 + (z + 1) % 4, y * 4 + (z + 3) % 4
    yp, ym = ((y + 1) % 4) * 4 + z, ((y + 3) % 4) * 4 + z

    barrier = pltpu.get_barrier_semaphore()
    for other in (zp, zm, yp, ym):
        pl.semaphore_signal(barrier, inc=1, device_id=(other, c), device_id_type=MESH)
    for d in range(1, COLS):
        pl.semaphore_signal(barrier, inc=1, device_id=(r, (c + d) % COLS), device_id_type=MESH)

    @pl.when(diag_src)
    def _():
        pl.semaphore_signal(barrier, inc=1, device_id=(out_row, k), device_id_type=MESH)

    @pl.when(diag_dst)
    def _():
        pl.semaphore_signal(barrier, inc=1, device_id=(r - 1, prev_col), device_id_type=MESH)

    def load_d(j):
        rows = span(j, PIECE)
        return pltpu.make_async_copy(diag_ref.at[rows], df.at[rows], dl_sem.at[j])

    def load_p(j):
        rows = span(j, PIECE)
        return pltpu.make_async_copy(panel_ref.at[rows], pf.at[rows], pl_sem.at[j])

    @pl.when(uses_d)
    def _():
        for j in range(8):
            load_d(j).start()

    for j in range(8):
        load_p(j).start()

    whole = DATES // CD * CD
    serp[:whole, :] = ser_ref[:whole, :]
    serp[whole:, :] = jnp.concatenate(
        [ser_ref[whole:, :], jnp.zeros((ALL - DATES, PIECE), F32)], axis=0)

    pl.semaphore_wait(barrier, 11 + diag_src.astype(jnp.int32) + diag_dst.astype(jnp.int32))

    def remote(src, dst, send, recv, device):
        return pltpu.make_async_remote_copy(
            src_ref=src, dst_ref=dst, send_sem=send, recv_sem=recv, device_id=device, device_id_type=MESH)

    def g_copy(src, i):
        return remote(serp.at[span(i, CD)], gbuf.at[src, i], gs_sem.at[i], gr_sem.at[src, i], (r, 7))

    def x_copy(e, i, row):
        part = xbuf.at[span(i, CD)]
        return remote(part, part, f_sem.at[e, i], x_sem.at[i], (row, c))

    def out_copy(i):
        return remote(obuf.at[i], xbuf.at[span(i, CD)], o_sem.at[i], x_sem.at[i], (out_row, k))

    def part_copy(i):
        return remote(obuf.at[i], pbuf.at[i], o_sem.at[i], p_sem.at[i], (r, next_col))

    def hand_copy(p, h):
        return remote(zbuf.at[p, h], zin.at[p, h], hs_sem.at[p, h], hr_sem.at[p, h], (r, c + 1 - 2 * core))

    def z_copy(p, h, q):
        return remote(zbuf.at[p, h, q], rbuf.at[chip, p], zs_sem.at[p, h, q], zr_sem.at[chip, p], (r, 4 * h + q))

    def z_wait(src, p):
        remote(zbuf.at[p, 0, 0], rbuf.at[src, p], zs_sem.at[p, 0, 0], zr_sem.at[src, p], (r, 2 * src + 1)).wait_recv()

    def s_copy(d):
        lane = pl.multiple_of((r % 2) * 512 + (d // 2) * 128, 128)
        return remote(xbuf.at[:, pl.ds(lane, 128)], sbuf, ss_sem.at[d], sr_sem, (r, d))

    edges = (
        (jnp.logical_and(dy == 0, dz <= 1), zp),
        (jnp.logical_and(dy == 0, dz == 0), zm),
        (dy <= 1, yp),
        (dy == 0, ym),
    )

    def send_out(i):
        @pl.when(final)
        def _():
            out_copy(i).start()

        @pl.when(jnp.logical_not(final))
        def _():
            part_copy(i).start()

    @pl.when(gives)
    def _():
        @pl.loop(0, CHUNKS)
        def _(i):
            g_copy(c, i).start()

    slot = step_ref[jnp.maximum(k, 0)] - 2 * r
    shift = r * (COLS * PIECE)

    def pick(first, second):
        return jnp.where(jnp.full(first.shape, slot, jnp.int32) == 0, first, second)

    def pick_rows(ref, j, size):
        return pick(ref[span(j, size), :], ref[pl.ds(pl.multiple_of(BS + j * size, size), size), :])

    def one_hot(row, first):
        pos = lax.broadcasted_iota(jnp.int32, (PIECE, 128), 0) + first
        return jnp.where(pos == row - shift, 1.0, 0.0).astype(BF16)

    @pl.when(uses_d)
    def _():
        @pl.loop(0, 8)
        def _(j):
            load_d(j).wait()

    @pl.when(jnp.logical_or(starts, two))
    def _():
        @pl.loop(0, 8)
        def _(j):
            hi, lo = split2(pick_rows(df, j, 128).T)
            dhi[:, span(j, 128)] = hi
            dlo[:, span(j, 128)] = lo

    @pl.when(starts)
    def _():
        for q in range(8):
            want = pick(idx_ref[q:q + 1, :], idx_ref[8 + q:9 + q, :])

            @pl.loop(0, COLS)
            def _(s):
                oh[span(s, PIECE), q * 128:(q + 1) * 128] = one_hot(want, s * PIECE)

        @pl.loop(0, CHUNKS)
        def _(i):
            hi, lo = split2(serp[span(i, CD), :])
            acc = nn(jnp.concatenate([hi, lo], axis=0), oh[7 * PIECE:, :])
            for s in range(7):
                g_copy(s, i).wait_recv()
                hi, lo = split2(gbuf[s, i])
                acc = acc + nn(jnp.concatenate([hi, lo], axis=0), oh[s * PIECE:(s + 1) * PIECE, :])

            @pl.when(k == 1)
            def _():
                obuf[i] = acc[:CD] + acc[CD:]

            @pl.when(k != 1)
            def _():
                both = acc.astype(BF16)
                obuf[i] = times(both[:CD], both[CD:], dhi[...], dlo[...])

            send_out(i)

    @pl.loop(0, 8)
    def _(j):
        load_p(j).wait()

    def turn_panel():
        @pl.loop(0, 8)
        def _(j):
            hi, lo = split2(pf[span(j, PIECE), :].T)
            phi[:, span(j, PIECE)] = hi
            plo[:, span(j, PIECE)] = lo

    @pl.when(jnp.logical_not(chain))
    def _():
        turn_panel()

    @pl.when(two)
    def _():
        @pl.loop(0, 8)
        def _(j):
            hi, lo = split2(pick_rows(pf, j, 128).T)
            mhi[:, span(j, 128)] = hi
            mlo[:, span(j, 128)] = lo

    @pl.when(jnp.logical_and(chain, k != 1))
    def _():
        @pl.loop(0, 8)
        def _(j):
            rows = span(j, 128)
            hi, lo = split2(pick_rows(df, j, 128))
            dhi[rows, :] = hi
            dlo[rows, :] = lo
            hi, lo = split2(pick_rows(pf, j, 128))
            oh[rows, :] = hi
            oh[pl.ds(pl.multiple_of(BS + j * 128, 128), 128), :] = lo

        @pl.loop(0, 4)
        def _(j):
            rows = span(j, PIECE)
            th = dhi[rows, :]
            ph = oh[:BS, :]
            m = nn(th, ph) + nn(dlo[rows, :], ph) + nn(th, oh[BS:, :])
            hi, lo = split2(m.T)
            mhi[:, rows] = hi
            mlo[:, rows] = lo

    for q in range(16):
        ohr[q // 2, :, q % 2 * 128:(q % 2 + 1) * 128] = one_hot(idx_ref[q:q + 1, :], c * PIECE)

    def half(p, h):
        hi, lo = split2(xbuf[span(p, PD), :])
        three = jnp.concatenate(split3(serp[span(p, PD), :]), axis=0)

        @pl.when(core == 1)
        def _():
            hand_copy(p, h).wait_recv()

        for q in range(4):
            d = 4 * h + q
            cols = span(d, PIECE)
            a = times(hi, lo, phi[:, cols], plo[:, cols])
            b = nn(three, ohr[d])
            v = b[:PD] + (b[PD:2 * PD] + b[2 * PD:]) - a

            @pl.when(core == 0)
            def _():
                zbuf[p, h, q] = v

            @pl.when(core == 1)
            def _():
                total = v + zin[p, h, q]

                @pl.when(d == c)
                def _():
                    rbuf[chip, p] = total

                @pl.when(d != c)
                def _():
                    zbuf[p, h, q] = total
                    z_copy(p, h, q).start()

        @pl.when(core == 0)
        def _():
            hand_copy(p, h).start()

    def arrive(i):
        x_copy(0, i, zp).wait_recv()
        for e, (cond, row) in enumerate(edges):
            @pl.when(cond)
            def _():
                x_copy(e, i, row).start()

    @pl.when(bulk)
    def _():
        @pl.loop(0, CHUNKS)
        def _(i):
            arrive(i)

            @pl.when(chain)
            def _():
                hi, lo = split2(xbuf[span(i, CD), :])
                a = times(hi, lo, mhi[...], mlo[...])
                part_copy(i).wait_recv()
                v = pbuf[i] - a

                @pl.when(two)
                def _():
                    vh, vl = split2(v)
                    obuf[i] = times(vh, vl, dhi[...], dlo[...])

                @pl.when(jnp.logical_not(two))
                def _():
                    obuf[i] = v

                send_out(i)

        @pl.when(chain)
        def _():
            turn_panel()

        @pl.loop(0, CHUNKS)
        def _(i):
            half(i // 2, i % 2)

    @pl.when(jnp.logical_not(bulk))
    def _():
        @pl.loop(0, CHUNKS + 2)
        def _(i):
            @pl.when(i < CHUNKS)
            def _():
                arrive(i)

            @pl.when(i >= 2)
            def _():
                half(i // 2 - 1, i % 2)

    def put_solved(v):
        t = v.T
        sol_ref[...] = jnp.where(jnp.full((64, DATES), core, jnp.int32) == 1, t[64:, :DATES], t[:64, :DATES])

    @pl.when(sol_src)
    def _():
        for d in range(COLS):
            @pl.when(d != c)
            def _():
                s_copy(d).start()
        lane = pl.multiple_of((r % 2) * 512 + chip * 128, 128)
        put_solved(xbuf[:, pl.ds(lane, 128)])

    @pl.when(jnp.logical_not(sol_src))
    def _():
        s_copy(c).wait_recv()
        put_solved(sbuf[...])

    @pl.loop(0, CHIPS)
    def _(s):
        @pl.when(jnp.logical_not(jnp.logical_and(core == 1, s == chip)))
        def _():
            @pl.loop(0, PAIRS)
            def _(p):
                z_wait(s, p)

    total = (rbuf[0] + rbuf[1]) + (rbuf[2] + rbuf[3])
    res_ref[...] = total.reshape(ALL, PIECE)[:DATES, :]

    @pl.loop(0, CHUNKS)
    def _(i):
        @pl.when(gives)
        def _():
            g_copy(c, i).wait_send()

        for e, (cond, row) in enumerate(edges):
            @pl.when(cond)
            def _():
                x_copy(e, i, row).wait_send()

        @pl.when(uses_d)
        def _():
            part_copy(i).wait_send()

        @pl.when(core == 0)
        def _():
            hand_copy(i // 2, i % 2).wait_send()

        @pl.when(core == 1)
        def _():
            for q in range(4):
                @pl.when(4 * (i % 2) + q != c)
                def _():
                    z_copy(i // 2, i % 2, q).wait_send()

    @pl.when(sol_src)
    def _():
        for d in range(COLS):
            @pl.when(d != c)
            def _():
                s_copy(d).wait_send()


def body(series, point_order, step_block, panel, diag_inverse):
    idx = point_order.reshape(16, 128)
    vmem = pl.BlockSpec(memory_space=pltpu.VMEM)
    hbm = pl.BlockSpec(memory_space=pl.ANY)
    dma = pltpu.SemaphoreType.DMA
    residual, solved = pl.pallas_call(
        kernel,
        out_shape=(
            jax.ShapeDtypeStruct((DATES, PIECE), F32),
            jax.ShapeDtypeStruct((64, DATES), F32),
        ),
        in_specs=[pl.BlockSpec(memory_space=pltpu.SMEM), vmem, vmem, hbm, hbm],
        out_specs=(vmem, vmem),
        scratch_shapes=[
            pltpu.VMEM((2 * BS, BS), F32),
            pltpu.VMEM((2 * BS, BS), F32),
            pltpu.VMEM((BS, 2 * BS), BF16),
            pltpu.VMEM((BS, 2 * BS), BF16),
            pltpu.VMEM((BS, BS), BF16),
            pltpu.VMEM((BS, BS), BF16),
            pltpu.VMEM((BS, BS), BF16),
            pltpu.VMEM((BS, BS), BF16),
            pltpu.VMEM((2 * BS, BS), BF16),
            pltpu.VMEM((COLS, PIECE, PIECE), BF16),
            pltpu.VMEM((ALL, PIECE), F32),
            pltpu.VMEM((7, CHUNKS, CD, PIECE), F32),
            pltpu.VMEM((ALL, BS), F32),
            pltpu.VMEM((CHUNKS, CD, BS), F32),
            pltpu.VMEM((CHUNKS, CD, BS), F32),
            pltpu.VMEM((PAIRS, 2, 4, PD, PIECE), F32),
            pltpu.VMEM((PAIRS, 2, 4, PD, PIECE), F32),
            pltpu.VMEM((CHIPS, PAIRS, PD, PIECE), F32),
            pltpu.VMEM((ALL, 128), F32),
            dma((8,)),
            dma((8,)),
            dma((CHUNKS,)),
            dma((7, CHUNKS)),
            dma((4, CHUNKS)),
            dma((CHUNKS,)),
            dma((CHUNKS,)),
            dma((CHUNKS,)),
            dma((PAIRS, 2, 4)),
            dma((CHIPS, PAIRS)),
            dma((PAIRS, 2)),
            dma((PAIRS, 2)),
            dma((COLS,)),
            dma,
        ],
        compiler_params=pltpu.CompilerParams(
            collective_id=0, has_side_effects=True, vmem_limit_bytes=60 * 1024 * 1024
        ),
    )(step_block, idx, series, panel, diag_inverse)
    return solved, residual.T


def solution(mesh):
    in_specs = (P(None, ("rows", "cols")), P("rows"), P(), P("rows", "cols"), P("rows", None))
    out_specs = (P(("rows", "cols"), None), P(("rows", "cols"), None))
    return jax.shard_map(body, mesh=mesh, in_specs=in_specs, out_specs=out_specs, check_vma=False)
```

time: 156 us -> 129 us (0.83); the launches traced: 156 us -> 127 us
  Pallas kernels: 148 us -> 123 us
  local copies, waits for them, and re-layouts: 6.49 us -> 3.25 us
    pallas_call x1, Pallas kernels: 148 us -> 123 us  [body(): pl.pallas_call(kernel, out_shape=(jax.ShapeDtypeStruct((DATES, PIECE), F3...]
    unnamed x1 -> x2, local copies, waits for them, and re-layouts: 0.76 us -> 3.25 us
    transpose x2 -> x0, local copies, waits for them, and re-layouts: 1.72 us -> none  [the longest x1 1.71 us: body(): residual = res.reshape(CHUNKS * CD, PIECE)[:dates].T]
    pad x1 -> x0, local copies, waits for them, and re-layouts: 1.7 us -> none  [body(): jnp.pad(series, ((0, CHUNKS * CD - dates), (0, 0)))]
where the time goes in v2:
time: 129 us; the launch traced here: 127 us
  Pallas kernels  123 us (95%)
  local copies, waits for them, and re-layouts  3.25 us (3%)
    pallas_call x1, Pallas kernels, body(): pl.pallas_call(kernel, out_shape=(jax.ShapeDtypeStruct((DATES, PIECE), F3...  123 us
    unnamed x2, local copies, waits for them, and re-layouts  3.25 us

profile of v2, /device:TPU:45, one launch (start us, length us, event | category | flops | bytes accessed | tf_op | source)
XLA Modules:
  0.0 126.8 jit_solution(18242767021303419529)
XLA Ops:
  0.6 122.9 %shard_map.68 = (f32[300,256]{1,0:T(8,128)}, f32[64,300]{1,0:T(8,128)}) custom-call(s32[8]{0:T(128)} %step_ref.1, s32[16,128]{1,0:T(8,128)} %bitcast.3, f32[300,256]{1,0:T(8,128)} %ser_ref.1, f32[2048,1024]{1,0:T(8,128)} %panel_ref.1, f32[2048,1024]{1,0:T(8,128)} %diag_ref.1), custom_call_target="tpu_custom_call" | custom-call | tf_op jit(solution)/shard_map/pallas_call | solution.py:427
  123.5 1.5 %copy.9 = f32[64,300]{1,0:T(8,128)} copy(f32[64,300]{1,0:T(8,128)} %get-tuple-element.8) | data formatting | bytes 153600
  125.1 1.7 %copy.10 = f32[256,300]{0,1:T(8,128)} copy(f32[256,300]{0,1:T(8,128)} %bitcast.2) | data formatting | bytes 614400

commit v3 on v2

--- a/solution.py
+++ b/solution.py
@@ -48,8 +48,8 @@
 
 
 def kernel(step_ref, idx_ref, ser_ref, panel_ref, diag_ref, res_ref, sol_ref,
-           pf, df, phi, plo, mhi, mlo, dhi, dlo, oh, ohr, serp, gbuf, xbuf, pbuf, obuf, zbuf, zin, rbuf, sbuf,
-           pl_sem, dl_sem, gs_sem, gr_sem, f_sem, x_sem, o_sem, p_sem, zs_sem, zr_sem, hs_sem, hr_sem, ss_sem, sr_sem):
+           pf, df, phi, plo, mhi, mlo, dhi, dlo, oh, ohr, serp, gbuf, xbuf, pin, abuf, obuf, zbuf, zin, rbuf, sbuf,
+           pl_sem, dl_sem, gs_sem, gr_sem, f_sem, x_sem, o_sem, far_sem, p_sem, a_sem, zs_sem, zr_sem, hs_sem, hr_sem, ss_sem, sr_sem):
     r = lax.axis_index("rows")
     c = lax.axis_index("cols")
     k = r - FIRST
@@ -63,14 +63,16 @@
     starts = jnp.logical_and(late, c == 7)
     gives = jnp.logical_and(late, c < 7)
     uses_d = jnp.logical_or(chain, starts)
-    two = jnp.logical_and(chain, k == 1)
     bulk = jnp.logical_and(late, 2 * chip < k)
     final = jnp.logical_and(late, c == (k + 15) % 8)
     diag_src = jnp.logical_and(final, r < 15)
     diag_dst = jnp.logical_and(c < 7, r == root)
+    far_src = jnp.logical_and(final, r < 14)
+    far_dst = jnp.logical_and(c < 6, r == root + 1)
+    far_row = jnp.minimum(r + 2, 15)
+    solver = jnp.maximum(k - 1, 0)
     out_row = jnp.minimum(r + 1, 15)
     prev_col = (c + 7) % 8
-    next_col = (c + 1) % 8
     sol_src = c == r // 2
 
     zp, zm = y * 4 + (z + 1) % 4, y * 4 + (z + 3) % 4
@@ -90,6 +92,14 @@
     def _():
         pl.semaphore_signal(barrier, inc=1, device_id=(r - 1, prev_col), device_id_type=MESH)
 
+    @pl.when(far_src)
+    def _():
+        pl.semaphore_signal(barrier, inc=1, device_id=(far_row, k), device_id_type=MESH)
+
+    @pl.when(far_dst)
+    def _():
+        pl.semaphore_signal(barrier, inc=1, device_id=(r - 2, prev_col), device_id_type=MESH)
+
     def load_d(j):
         rows = span(j, PIECE)
         return pltpu.make_async_copy(diag_ref.at[rows], df.at[rows], dl_sem.at[j])
@@ -111,14 +121,17 @@
     serp[whole:, :] = jnp.concatenate(
         [ser_ref[whole:, :], jnp.zeros((ALL - DATES, PIECE), F32)], axis=0)
 
-    pl.semaphore_wait(barrier, 11 + diag_src.astype(jnp.int32) + diag_dst.astype(jnp.int32))
+    one = jnp.int32(1)
+    zero = jnp.int32(0)
+    extra = sum(jnp.where(cond, one, zero) for cond in (diag_src, diag_dst, far_src, far_dst))
+    pl.semaphore_wait(barrier, 11 + extra)
 
     def remote(src, dst, send, recv, device):
         return pltpu.make_async_remote_copy(
             src_ref=src, dst_ref=dst, send_sem=send, recv_sem=recv, device_id=device, device_id_type=MESH)
 
     def g_copy(src, i):
-        return remote(serp.at[span(i, CD)], gbuf.at[src, i], gs_sem.at[i], gr_sem.at[src, i], (r, 7))
+        return remote(serp.at[span(i, CD)], gbuf.at[src, span(i, CD)], gs_sem.at[i], gr_sem.at[src, i], (r, 7))
 
     def x_copy(e, i, row):
         part = xbuf.at[span(i, CD)]
@@ -127,8 +140,14 @@
     def out_copy(i):
         return remote(obuf.at[i], xbuf.at[span(i, CD)], o_sem.at[i], x_sem.at[i], (out_row, k))
 
-    def part_copy(i):
-        return remote(obuf.at[i], pbuf.at[i], o_sem.at[i], p_sem.at[i], (r, next_col))
+    def far_copy(i):
+        return remote(obuf.at[i], xbuf.at[span(i, CD)], far_sem.at[i], x_sem.at[i], (far_row, k))
+
+    def pair_copy(i):
+        return remote(obuf.at[i], pin.at[i], o_sem.at[i], p_sem.at[i], (r, c + 1 - 2 * core))
+
+    def sum_copy(s, i):
+        return remote(obuf.at[i], abuf.at[s, i], o_sem.at[i], a_sem.at[s, i], (r, solver))
 
     def hand_copy(p, h):
         return remote(zbuf.at[p, h], zin.at[p, h], hs_sem.at[p, h], hr_sem.at[p, h], (r, c + 1 - 2 * core))
@@ -143,10 +162,12 @@
         lane = pl.multiple_of((r % 2) * 512 + (d // 2) * 128, 128)
         return remote(xbuf.at[:, pl.ds(lane, 128)], sbuf, ss_sem.at[d], sr_sem, (r, d))
 
+    skip_z = jnp.logical_and(r == root, jnp.logical_and(c < 6, c != 2))
+    skip_y = jnp.logical_and(r == FIRST, c == 2)
     edges = (
-        (jnp.logical_and(dy == 0, dz <= 1), zp),
+        (jnp.logical_and(jnp.logical_and(dy == 0, dz <= 1), jnp.logical_not(skip_z)), zp),
         (jnp.logical_and(dy == 0, dz == 0), zm),
-        (dy <= 1, yp),
+        (jnp.logical_and(dy <= 1, jnp.logical_not(skip_y)), yp),
         (dy == 0, ym),
     )
 
@@ -155,9 +176,19 @@
         def _():
             out_copy(i).start()
 
+            @pl.when(far_src)
+            def _():
+                far_copy(i).start()
+
         @pl.when(jnp.logical_not(final))
         def _():
-            part_copy(i).start()
+            @pl.when(jnp.logical_and(chain, core == 0))
+            def _():
+                pair_copy(i).start()
+
+            @pl.when(core == 1)
+            def _():
+                sum_copy(chip, i).start()
 
     @pl.when(gives)
     def _():
@@ -184,7 +215,7 @@
         def _(j):
             load_d(j).wait()
 
-    @pl.when(jnp.logical_or(starts, two))
+    @pl.when(starts)
     def _():
         @pl.loop(0, 8)
         def _(j):
@@ -201,25 +232,21 @@
             def _(s):
                 oh[span(s, PIECE), q * 128:(q + 1) * 128] = one_hot(want, s * PIECE)
 
-        @pl.loop(0, CHUNKS)
-        def _(i):
-            hi, lo = split2(serp[span(i, CD), :])
+        @pl.loop(0, PAIRS)
+        def _(p):
+            hi, lo = split2(serp[span(p, PD), :])
             acc = nn(jnp.concatenate([hi, lo], axis=0), oh[7 * PIECE:, :])
             for s in range(7):
-                g_copy(s, i).wait_recv()
-                hi, lo = split2(gbuf[s, i])
+                g_copy(s, 2 * p).wait_recv()
+                g_copy(s, 2 * p + 1).wait_recv()
+                hi, lo = split2(gbuf[s, span(p, PD), :])
                 acc = acc + nn(jnp.concatenate([hi, lo], axis=0), oh[s * PIECE:(s + 1) * PIECE, :])
-
-            @pl.when(k == 1)
-            def _():
-                obuf[i] = acc[:CD] + acc[CD:]
-
-            @pl.when(k != 1)
-            def _():
-                both = acc.astype(BF16)
-                obuf[i] = times(both[:CD], both[CD:], dhi[...], dlo[...])
-
-            send_out(i)
+            both = acc.astype(BF16)
+            v = times(both[:PD], both[PD:], dhi[...], dlo[...])
+            obuf[2 * p] = v[:CD]
+            obuf[2 * p + 1] = v[CD:]
+            send_out(2 * p)
+            send_out(2 * p + 1)
 
     @pl.loop(0, 8)
     def _(j):
@@ -232,19 +259,7 @@
             phi[:, span(j, PIECE)] = hi
             plo[:, span(j, PIECE)] = lo
 
-    @pl.when(jnp.logical_not(chain))
-    def _():
-        turn_panel()
-
-    @pl.when(two)
-    def _():
-        @pl.loop(0, 8)
-        def _(j):
-            hi, lo = split2(pick_rows(pf, j, 128).T)
-            mhi[:, span(j, 128)] = hi
-            mlo[:, span(j, 128)] = lo
-
-    @pl.when(jnp.logical_and(chain, k != 1))
+    @pl.when(chain)
     def _():
         @pl.loop(0, 8)
         def _(j):
@@ -266,6 +281,12 @@
             mhi[:, rows] = hi
             mlo[:, rows] = lo
 
+    late_turn = jnp.logical_and(chain, k <= 2)
+
+    @pl.when(jnp.logical_not(late_turn))
+    def _():
+        turn_panel()
+
     for q in range(16):
         ohr[q // 2, :, q % 2 * 128:(q % 2 + 1) * 128] = one_hot(idx_ref[q:q + 1, :], c * PIECE)
 
@@ -307,10 +328,14 @@
 
     def arrive(i):
         x_copy(0, i, zp).wait_recv()
+
+    def forward(i):
         for e, (cond, row) in enumerate(edges):
             @pl.when(cond)
             def _():
                 x_copy(e, i, row).start()
+
+    solves = jnp.logical_and(chain, final)
 
     @pl.when(bulk)
     def _():
@@ -318,25 +343,37 @@
         def _(i):
             arrive(i)
 
+            @pl.when(jnp.logical_not(solves))
+            def _():
+                forward(i)
+
             @pl.when(chain)
             def _():
                 hi, lo = split2(xbuf[span(i, CD), :])
-                a = times(hi, lo, mhi[...], mlo[...])
-                part_copy(i).wait_recv()
-                v = pbuf[i] - a
-
-                @pl.when(two)
+                obuf[i] = times(hi, lo, mhi[...], mlo[...])
+
+                @pl.when(core == 1)
                 def _():
-                    vh, vl = split2(v)
-                    obuf[i] = times(vh, vl, dhi[...], dlo[...])
-
-                @pl.when(jnp.logical_not(two))
+                    pair_copy(i).wait_recv()
+                    obuf[i] = obuf[i] + pin[i]
+
+                @pl.when(final)
                 def _():
-                    obuf[i] = v
+                    for s in range(CHIPS - 1):
+                        @pl.when(s < chip)
+                        def _():
+                            sum_copy(s, i).wait_recv()
+                            obuf[i] = obuf[i] + abuf[s, i]
+                    sum_copy(3, i).wait_recv()
+                    obuf[i] = abuf[3, i] - obuf[i]
 
                 send_out(i)
 
-        @pl.when(chain)
+            @pl.when(solves)
+            def _():
+                forward(i)
+
+        @pl.when(late_turn)
         def _():
             turn_panel()
 
@@ -351,6 +388,7 @@
             @pl.when(i < CHUNKS)
             def _():
                 arrive(i)
+                forward(i)
 
             @pl.when(i >= 2)
             def _():
@@ -398,7 +436,11 @@
 
         @pl.when(uses_d)
         def _():
-            part_copy(i).wait_send()
+            pair_copy(i).wait_send()
+
+        @pl.when(far_src)
+        def _():
+            far_copy(i).wait_send()
 
         @pl.when(core == 0)
         def _():
@@ -444,9 +486,10 @@
             pltpu.VMEM((2 * BS, BS), BF16),
             pltpu.VMEM((COLS, PIECE, PIECE), BF16),
             pltpu.VMEM((ALL, PIECE), F32),
-            pltpu.VMEM((7, CHUNKS, CD, PIECE), F32),
+            pltpu.VMEM((7, ALL, PIECE), F32),
             pltpu.VMEM((ALL, BS), F32),
             pltpu.VMEM((CHUNKS, CD, BS), F32),
+            pltpu.VMEM((CHIPS, CHUNKS, CD, BS), F32),
             pltpu.VMEM((CHUNKS, CD, BS), F32),
             pltpu.VMEM((PAIRS, 2, 4, PD, PIECE), F32),
             pltpu.VMEM((PAIRS, 2, 4, PD, PIECE), F32),
@@ -460,6 +503,8 @@
             dma((CHUNKS,)),
             dma((CHUNKS,)),
             dma((CHUNKS,)),
+            dma((CHUNKS,)),
+            dma((CHIPS, CHUNKS)),
             dma((PAIRS, 2, 4)),
             dma((CHIPS, PAIRS)),
             dma((PAIRS, 2)),

time: 129 us -> 135 us (1.047); the launches traced: 127 us -> 135 us
  Pallas kernels: 123 us -> 131 us
    pallas_call x1, Pallas kernels: 123 us -> 131 us  [body(): pl.pallas_call(kernel, out_shape=(jax.ShapeDtypeStruct((DATES, PIECE), F3...]
where the time goes in v3:
time: 135 us
  Pallas kernels  131 us (97%)
  local copies, waits for them, and re-layouts  3.25 us (2%)
    pallas_call x1, Pallas kernels, body(): pl.pallas_call(kernel, out_shape=(jax.ShapeDtypeStruct((DATES, PIECE), F3...  131 us
    unnamed x2, local copies, waits for them, and re-layouts  3.25 us

profile of v3, /device:TPU:45, one launch (start us, length us, event | category | flops | bytes accessed | tf_op | source)
XLA Modules:
  0.0 135.0 jit_solution(5257363912334301535)
XLA Ops:
  0.6 131.1 %shard_map.68 = (f32[300,256]{1,0:T(8,128)}, f32[64,300]{1,0:T(8,128)}) custom-call(s32[8]{0:T(128)} %step_ref.1, s32[16,128]{1,0:T(8,128)} %bitcast.3, f32[300,256]{1,0:T(8,128)} %ser_ref.1, f32[2048,1024]{1,0:T(8,128)} %panel_ref.1, f32[2048,1024]{1,0:T(8,128)} %diag_ref.1), custom_call_target="tpu_custom_call" | custom-call | tf_op jit(solution)/shard_map/pallas_call | solution.py:469
  131.7 1.5 %copy.9 = f32[64,300]{1,0:T(8,128)} copy(f32[64,300]{1,0:T(8,128)} %get-tuple-element.8) | data formatting | bytes 153600
  133.3 1.7 %copy.10 = f32[256,300]{0,1:T(8,128)} copy(f32[256,300]{0,1:T(8,128)} %bitcast.2) | data formatting | bytes 614400

commit v4 on v3

--- a/solution.py
+++ b/solution.py
@@ -49,7 +49,7 @@
 
 def kernel(step_ref, idx_ref, ser_ref, panel_ref, diag_ref, res_ref, sol_ref,
            pf, df, phi, plo, mhi, mlo, dhi, dlo, oh, ohr, serp, gbuf, xbuf, pin, abuf, obuf, zbuf, zin, rbuf, sbuf,
-           pl_sem, dl_sem, gs_sem, gr_sem, f_sem, x_sem, o_sem, far_sem, p_sem, a_sem, zs_sem, zr_sem, hs_sem, hr_sem, ss_sem, sr_sem):
+           pl_sem, dl_sem, gs_sem, gr_sem, f_sem, x_sem, o_sem, v_sem, p_sem, a_sem, zs_sem, zr_sem, hs_sem, hr_sem, ss_sem, sr_sem):
     r = lax.axis_index("rows")
     c = lax.axis_index("cols")
     k = r - FIRST
@@ -67,10 +67,17 @@
     final = jnp.logical_and(late, c == (k + 15) % 8)
     diag_src = jnp.logical_and(final, r < 15)
     diag_dst = jnp.logical_and(c < 7, r == root)
-    far_src = jnp.logical_and(final, r < 14)
-    far_dst = jnp.logical_and(c < 6, r == root + 1)
-    far_row = jnp.minimum(r + 2, 15)
     solver = jnp.maximum(k - 1, 0)
+    solver_chip = solver // 2
+    near = jnp.logical_or(chip + 1 == solver_chip, jnp.logical_or(c == 7, jnp.logical_and(chip == 0, solver_chip == 3)))
+    sum_col = jnp.where(near, solver, jnp.minimum(c + 2, 7))
+    takes = jnp.logical_and(jnp.logical_and(chain, core == 1), jnp.logical_and(chip >= 1, chip + 1 == solver_chip))
+    via_src = jnp.logical_or(jnp.logical_and(r == 8, c == 7), jnp.logical_and(r == 12, c == 3))
+    via_dev = jnp.logical_or(jnp.logical_and(r == 10, c == 6), jnp.logical_and(r == 14, c == 7))
+    via_row = jnp.minimum(r + 2, 15)
+    via_col = jnp.where(r == 8, 6, 7)
+    via_from = jnp.where(r == 10, 7, 3)
+    via_to = jnp.where(r == 10, 0, 4)
     out_row = jnp.minimum(r + 1, 15)
     prev_col = (c + 7) % 8
     sol_src = c == r // 2
@@ -92,13 +99,13 @@
     def _():
         pl.semaphore_signal(barrier, inc=1, device_id=(r - 1, prev_col), device_id_type=MESH)
 
-    @pl.when(far_src)
-    def _():
-        pl.semaphore_signal(barrier, inc=1, device_id=(far_row, k), device_id_type=MESH)
-
-    @pl.when(far_dst)
-    def _():
-        pl.semaphore_signal(barrier, inc=1, device_id=(r - 2, prev_col), device_id_type=MESH)
+    @pl.when(via_src)
+    def _():
+        pl.semaphore_signal(barrier, inc=1, device_id=(via_row, via_col), device_id_type=MESH)
+
+    @pl.when(via_dev)
+    def _():
+        pl.semaphore_signal(barrier, inc=1, device_id=(jnp.maximum(r - 2, 0), via_from), device_id_type=MESH)
 
     def load_d(j):
         rows = span(j, PIECE)
@@ -123,7 +130,7 @@
 
     one = jnp.int32(1)
     zero = jnp.int32(0)
-    extra = sum(jnp.where(cond, one, zero) for cond in (diag_src, diag_dst, far_src, far_dst))
+    extra = sum(jnp.where(cond, one, zero) for cond in (diag_src, diag_dst, via_src, via_dev))
     pl.semaphore_wait(barrier, 11 + extra)
 
     def remote(src, dst, send, recv, device):
@@ -140,14 +147,17 @@
     def out_copy(i):
         return remote(obuf.at[i], xbuf.at[span(i, CD)], o_sem.at[i], x_sem.at[i], (out_row, k))
 
-    def far_copy(i):
-        return remote(obuf.at[i], xbuf.at[span(i, CD)], far_sem.at[i], x_sem.at[i], (far_row, k))
+    def via_copy(i):
+        return remote(obuf.at[i], abuf.at[0, i], v_sem.at[i], a_sem.at[0, i], (via_row, via_col))
+
+    def hop_copy(i):
+        return remote(abuf.at[0, i], xbuf.at[span(i, CD)], v_sem.at[i], x_sem.at[i], (r, via_to))
 
     def pair_copy(i):
         return remote(obuf.at[i], pin.at[i], o_sem.at[i], p_sem.at[i], (r, c + 1 - 2 * core))
 
     def sum_copy(s, i):
-        return remote(obuf.at[i], abuf.at[s, i], o_sem.at[i], a_sem.at[s, i], (r, solver))
+        return remote(obuf.at[i], abuf.at[s, i], o_sem.at[i], a_sem.at[s, i], (r, sum_col))
 
     def hand_copy(p, h):
         return remote(zbuf.at[p, h], zin.at[p, h], hs_sem.at[p, h], hr_sem.at[p, h], (r, c + 1 - 2 * core))
@@ -162,13 +172,15 @@
         lane = pl.multiple_of((r % 2) * 512 + (d // 2) * 128, 128)
         return remote(xbuf.at[:, pl.ds(lane, 128)], sbuf, ss_sem.at[d], sr_sem, (r, d))
 
-    skip_z = jnp.logical_and(r == root, jnp.logical_and(c < 6, c != 2))
-    skip_y = jnp.logical_and(r == FIRST, c == 2)
+    turned = c == 7
+    on_z = jnp.logical_or(turned, dy == 0)
+    on_y = jnp.logical_or(jnp.logical_not(turned), dz == 0)
+    served = jnp.logical_and(r == root, jnp.logical_or(c == 0, c == 4))
     edges = (
-        (jnp.logical_and(jnp.logical_and(dy == 0, dz <= 1), jnp.logical_not(skip_z)), zp),
-        (jnp.logical_and(dy == 0, dz == 0), zm),
-        (jnp.logical_and(dy <= 1, jnp.logical_not(skip_y)), yp),
-        (dy == 0, ym),
+        (jnp.logical_and(jnp.logical_and(on_z, dz <= 1), jnp.logical_not(served)), zp),
+        (jnp.logical_and(on_z, dz == 0), zm),
+        (jnp.logical_and(on_y, dy <= 1), yp),
+        (jnp.logical_and(on_y, dy == 0), ym),
     )
 
     def send_out(i):
@@ -176,9 +188,9 @@
         def _():
             out_copy(i).start()
 
-            @pl.when(far_src)
-            def _():
-                far_copy(i).start()
+            @pl.when(via_src)
+            def _():
+                via_copy(i).start()
 
         @pl.when(jnp.logical_not(final))
         def _():
@@ -192,9 +204,15 @@
 
     @pl.when(gives)
     def _():
-        @pl.loop(0, CHUNKS)
-        def _(i):
-            g_copy(c, i).start()
+        @pl.loop(0, PAIRS)
+        def _(p):
+            g_copy(c, 2 * p).start()
+            g_copy(c, 2 * p + 1).start()
+
+            @pl.when(r == FIRST)
+            def _():
+                g_copy(c, 2 * p).wait_send()
+                g_copy(c, 2 * p + 1).wait_send()
 
     slot = step_ref[jnp.maximum(k, 0)] - 2 * r
     shift = r * (COLS * PIECE)
@@ -329,13 +347,20 @@
     def arrive(i):
         x_copy(0, i, zp).wait_recv()
 
-    def forward(i):
-        for e, (cond, row) in enumerate(edges):
+    def forward(i, first=0, last=4):
+        for e, (cond, row) in list(enumerate(edges))[first:last]:
             @pl.when(cond)
             def _():
                 x_copy(e, i, row).start()
 
     solves = jnp.logical_and(chain, final)
+
+    @pl.when(via_dev)
+    def _():
+        @pl.loop(0, CHUNKS)
+        def _(i):
+            sum_copy(0, i).wait_recv()
+            hop_copy(i).start()
 
     @pl.when(bulk)
     def _():
@@ -343,9 +368,11 @@
         def _(i):
             arrive(i)
 
+            forward(i, 0, 1)
+
             @pl.when(jnp.logical_not(solves))
             def _():
-                forward(i)
+                forward(i, 1, 4)
 
             @pl.when(chain)
             def _():
@@ -357,10 +384,15 @@
                     pair_copy(i).wait_recv()
                     obuf[i] = obuf[i] + pin[i]
 
+                @pl.when(takes)
+                def _():
+                    sum_copy(chip - 1, i).wait_recv()
+                    obuf[i] = obuf[i] + abuf[chip - 1, i]
+
                 @pl.when(final)
                 def _():
                     for s in range(CHIPS - 1):
-                        @pl.when(s < chip)
+                        @pl.when(jnp.logical_or(s == chip - 1, jnp.logical_and(s == 0, chip == 3)))
                         def _():
                             sum_copy(s, i).wait_recv()
                             obuf[i] = obuf[i] + abuf[s, i]
@@ -371,7 +403,7 @@
 
             @pl.when(solves)
             def _():
-                forward(i)
+                forward(i, 1, 4)
 
         @pl.when(late_turn)
         def _():
@@ -425,7 +457,7 @@
 
     @pl.loop(0, CHUNKS)
     def _(i):
-        @pl.when(gives)
+        @pl.when(jnp.logical_and(gives, r != FIRST))
         def _():
             g_copy(c, i).wait_send()
 
@@ -438,9 +470,9 @@
         def _():
             pair_copy(i).wait_send()
 
-        @pl.when(far_src)
-        def _():
-            far_copy(i).wait_send()
+        @pl.when(jnp.logical_or(via_src, via_dev))
+        def _():
+            via_copy(i).wait_send()
 
         @pl.when(core == 0)
         def _():

time: 135 us -> 125 us (0.926)
  Pallas kernels: 131 us -> 121 us
    pallas_call x1, Pallas kernels: 131 us -> 121 us  [body(): pl.pallas_call(kernel, out_shape=(jax.ShapeDtypeStruct((DATES, PIECE), F3...]
where the time goes in v4:
time: 125 us
  Pallas kernels  121 us (97%)
  local copies, waits for them, and re-layouts  3.25 us (3%)
    pallas_call x1, Pallas kernels, body(): pl.pallas_call(kernel, out_shape=(jax.ShapeDtypeStruct((DATES, PIECE), F3...  121 us
    unnamed x2, local copies, waits for them, and re-layouts  3.25 us

profile of v4, /device:TPU:45, one launch (start us, length us, event | category | flops | bytes accessed | tf_op | source)
XLA Modules:
  0.0 124.8 jit_solution(2419500207173927865)
XLA Ops:
  0.6 120.9 %shard_map.68 = (f32[300,256]{1,0:T(8,128)}, f32[64,300]{1,0:T(8,128)}) custom-call(s32[8]{0:T(128)} %step_ref.1, s32[16,128]{1,0:T(8,128)} %bitcast.3, f32[300,256]{1,0:T(8,128)} %ser_ref.1, f32[2048,1024]{1,0:T(8,128)} %panel_ref.1, f32[2048,1024]{1,0:T(8,128)} %diag_ref.1), custom_call_target="tpu_custom_call" | custom-call | tf_op jit(solution)/shard_map/pallas_call | solution.py:501
  121.5 1.5 %copy.9 = f32[64,300]{1,0:T(8,128)} copy(f32[64,300]{1,0:T(8,128)} %get-tuple-element.8) | data formatting | bytes 153600
  123.0 1.7 %copy.10 = f32[256,300]{0,1:T(8,128)} copy(f32[256,300]{0,1:T(8,128)} %bitcast.2) | data formatting | bytes 614400

commit v5 on v4

--- a/solution.py
+++ b/solution.py
@@ -176,10 +176,15 @@
     on_z = jnp.logical_or(turned, dy == 0)
     on_y = jnp.logical_or(jnp.logical_not(turned), dz == 0)
     served = jnp.logical_and(r == root, jnp.logical_or(c == 0, c == 4))
+    even = core == 0
+    ahead = jnp.logical_or(dz == 0, jnp.logical_and(jnp.logical_not(even), dz == 1))
+    behind = jnp.logical_or(dz == 0, jnp.logical_and(even, dz == 3))
+    bend = jnp.logical_and(c == 2, r == 14)
+    bare = jnp.logical_and(c == 2, r == root)
     edges = (
-        (jnp.logical_and(jnp.logical_and(on_z, dz <= 1), jnp.logical_not(served)), zp),
-        (jnp.logical_and(on_z, dz == 0), zm),
-        (jnp.logical_and(on_y, dy <= 1), yp),
+        (jnp.logical_or(bend, jnp.logical_and(jnp.logical_and(on_z, ahead), jnp.logical_not(served))), zp),
+        (jnp.logical_and(on_z, behind), zm),
+        (jnp.logical_and(jnp.logical_and(on_y, dy <= 1), jnp.logical_not(bare)), yp),
         (jnp.logical_and(on_y, dy == 0), ym),
     )
 
@@ -368,11 +373,11 @@
         def _(i):
             arrive(i)
 
-            forward(i, 0, 1)
+            forward(i, 0, 2)
 
             @pl.when(jnp.logical_not(solves))
             def _():
-                forward(i, 1, 4)
+                forward(i, 2, 4)
 
             @pl.when(chain)
             def _():
@@ -403,7 +408,7 @@
 
             @pl.when(solves)
             def _():
-                forward(i, 1, 4)
+                forward(i, 2, 4)
 
         @pl.when(late_turn)
         def _():

time: 125 us -> 122 us (0.976)
  Pallas kernels: 121 us -> 117 us
    pallas_call x1, Pallas kernels: 121 us -> 117 us  [body(): pl.pallas_call(kernel, out_shape=(jax.ShapeDtypeStruct((DATES, PIECE), F3...]
where the time goes in v5:
time: 122 us; the launch traced here: 121 us
  Pallas kernels  117 us (96%)
  local copies, waits for them, and re-layouts  3.25 us (3%)
    pallas_call x1, Pallas kernels, body(): pl.pallas_call(kernel, out_shape=(jax.ShapeDtypeStruct((DATES, PIECE), F3...  117 us
    unnamed x2, local copies, waits for them, and re-layouts  3.25 us

profile of v5, /device:TPU:45, one launch (start us, length us, event | category | flops | bytes accessed | tf_op | source)
XLA Modules:
  0.0 121.2 jit_solution(14414480231842369247)
XLA Ops:
  0.6 117.3 %shard_map.68 = (f32[300,256]{1,0:T(8,128)}, f32[64,300]{1,0:T(8,128)}) custom-call(s32[8]{0:T(128)} %step_ref.1, s32[16,128]{1,0:T(8,128)} %bitcast.3, f32[300,256]{1,0:T(8,128)} %ser_ref.1, f32[2048,1024]{1,0:T(8,128)} %panel_ref.1, f32[2048,1024]{1,0:T(8,128)} %diag_ref.1), custom_call_target="tpu_custom_call" | custom-call | tf_op jit(solution)/shard_map/pallas_call | solution.py:506
  118.0 1.5 %copy.9 = f32[64,300]{1,0:T(8,128)} copy(f32[64,300]{1,0:T(8,128)} %get-tuple-element.8) | data formatting | bytes 153600
  119.5 1.7 %copy.10 = f32[256,300]{0,1:T(8,128)} copy(f32[256,300]{0,1:T(8,128)} %bitcast.2) | data formatting | bytes 614400

commit v6 on v5

--- a/solution.py
+++ b/solution.py
@@ -11,6 +11,7 @@
 DATES = 300
 CHUNKS = 10
 CD = 32
+LAST = 16
 PAIRS = CHUNKS // 2
 PD = 2 * CD
 ALL = CHUNKS * CD
@@ -63,7 +64,7 @@
     starts = jnp.logical_and(late, c == 7)
     gives = jnp.logical_and(late, c < 7)
     uses_d = jnp.logical_or(chain, starts)
-    bulk = jnp.logical_and(late, 2 * chip < k)
+    bulk = jnp.logical_and(jnp.logical_and(late, 2 * chip < k), jnp.logical_not(jnp.logical_and(r == 15, c == 7)))
     final = jnp.logical_and(late, c == (k + 15) % 8)
     diag_src = jnp.logical_and(final, r < 15)
     diag_dst = jnp.logical_and(c < 7, r == root)
@@ -128,11 +129,37 @@
     serp[whole:, :] = jnp.concatenate(
         [ser_ref[whole:, :], jnp.zeros((ALL - DATES, PIECE), F32)], axis=0)
 
+    xbuf[ALL - LAST:, :] = jnp.zeros((LAST, BS), F32)
     one = jnp.int32(1)
     zero = jnp.int32(0)
     extra = sum(jnp.where(cond, one, zero) for cond in (diag_src, diag_dst, via_src, via_dev))
     pl.semaphore_wait(barrier, 11 + extra)
 
+    class Sized:
+        def __init__(self, make, i):
+            self.make, self.i = make, i
+
+        def each(self, act):
+            @pl.when(self.i < CHUNKS - 1)
+            def _():
+                act(self.make(CD))
+
+            @pl.when(self.i == CHUNKS - 1)
+            def _():
+                act(self.make(LAST))
+
+        def start(self):
+            self.each(lambda copy: copy.start())
+
+        def wait_send(self):
+            self.each(lambda copy: copy.wait_send())
+
+        def wait_recv(self):
+            self.each(lambda copy: copy.wait_recv())
+
+    def rows_of(i, n):
+        return pl.ds(pl.multiple_of(i * CD, CD), n)
+
     def remote(src, dst, send, recv, device):
         return pltpu.make_async_remote_copy(
             src_ref=src, dst_ref=dst, send_sem=send, recv_sem=recv, device_id=device, device_id_type=MESH)
@@ -141,23 +168,30 @@
         return remote(serp.at[span(i, CD)], gbuf.at[src, span(i, CD)], gs_sem.at[i], gr_sem.at[src, i], (r, 7))
 
     def x_copy(e, i, row):
-        part = xbuf.at[span(i, CD)]
-        return remote(part, part, f_sem.at[e, i], x_sem.at[i], (row, c))
+        def make(n):
+            part = xbuf.at[rows_of(i, n)]
+            return remote(part, part, f_sem.at[e, i], x_sem.at[i], (row, c))
+        return Sized(make, i)
 
     def out_copy(i):
-        return remote(obuf.at[i], xbuf.at[span(i, CD)], o_sem.at[i], x_sem.at[i], (out_row, k))
+        return Sized(lambda n: remote(
+            obuf.at[i, pl.ds(0, n)], xbuf.at[rows_of(i, n)], o_sem.at[i], x_sem.at[i], (out_row, k)), i)
 
     def via_copy(i):
-        return remote(obuf.at[i], abuf.at[0, i], v_sem.at[i], a_sem.at[0, i], (via_row, via_col))
+        return Sized(lambda n: remote(
+            obuf.at[i, pl.ds(0, n)], abuf.at[0, i, pl.ds(0, n)], v_sem.at[i], a_sem.at[0, i], (via_row, via_col)), i)
 
     def hop_copy(i):
-        return remote(abuf.at[0, i], xbuf.at[span(i, CD)], v_sem.at[i], x_sem.at[i], (r, via_to))
+        return Sized(lambda n: remote(
+            abuf.at[0, i, pl.ds(0, n)], xbuf.at[rows_of(i, n)], v_sem.at[i], x_sem.at[i], (r, via_to)), i)
 
     def pair_copy(i):
-        return remote(obuf.at[i], pin.at[i], o_sem.at[i], p_sem.at[i], (r, c + 1 - 2 * core))
+        return Sized(lambda n: remote(
+            obuf.at[i, pl.ds(0, n)], pin.at[i, pl.ds(0, n)], o_sem.at[i], p_sem.at[i], (r, c + 1 - 2 * core)), i)
 
     def sum_copy(s, i):
-        return remote(obuf.at[i], abuf.at[s, i], o_sem.at[i], a_sem.at[s, i], (r, sum_col))
+        return Sized(lambda n: remote(
+            obuf.at[i, pl.ds(0, n)], abuf.at[s, i, pl.ds(0, n)], o_sem.at[i], a_sem.at[s, i], (r, sum_col)), i)
 
     def hand_copy(p, h):
         return remote(zbuf.at[p, h], zin.at[p, h], hs_sem.at[p, h], hr_sem.at[p, h], (r, c + 1 - 2 * core))
@@ -359,6 +393,7 @@
                 x_copy(e, i, row).start()
 
     solves = jnp.logical_and(chain, final)
+    early = jnp.logical_and(r == 15, c == 6)
 
     @pl.when(via_dev)
     def _():
@@ -410,11 +445,15 @@
             def _():
                 forward(i, 2, 4)
 
+            @pl.when(jnp.logical_and(early, i >= 2))
+            def _():
+                half(i // 2 - 1, i % 2)
+
         @pl.when(late_turn)
         def _():
             turn_panel()
 
-        @pl.loop(0, CHUNKS)
+        @pl.loop(jnp.where(early, CHUNKS - 2, 0), CHUNKS)
         def _(i):
             half(i // 2, i % 2)
 

time: 122 us -> 122 us (level)
  no operation moved by 1% of the time
where the time goes in v6:
time: 122 us
  Pallas kernels  118 us (97%)
  local copies, waits for them, and re-layouts  3.25 us (3%)
    pallas_call x1, Pallas kernels, body(): pl.pallas_call(kernel, out_shape=(jax.ShapeDtypeStruct((DATES, PIECE), F3...  118 us
    unnamed x2, local copies, waits for them, and re-layouts  3.25 us

profile of v6, /device:TPU:45, one launch (start us, length us, event | category | flops | bytes accessed | tf_op | source)
XLA Modules:
  0.0 121.5 jit_solution(18018841867362899681)
XLA Ops:
  0.6 117.7 %shard_map.68 = (f32[300,256]{1,0:T(8,128)}, f32[64,300]{1,0:T(8,128)}) custom-call(s32[8]{0:T(128)} %step_ref.1, s32[16,128]{1,0:T(8,128)} %bitcast.3, f32[300,256]{1,0:T(8,128)} %ser_ref.1, f32[2048,1024]{1,0:T(8,128)} %panel_ref.1, f32[2048,1024]{1,0:T(8,128)} %diag_ref.1), custom_call_target="tpu_custom_call" | custom-call | tf_op jit(solution)/shard_map/pallas_call | solution.py:545
  118.3 1.5 %copy.9 = f32[64,300]{1,0:T(8,128)} copy(f32[64,300]{1,0:T(8,128)} %get-tuple-element.8) | data formatting | bytes 153600
  119.8 1.7 %copy.10 = f32[256,300]{0,1:T(8,128)} copy(f32[256,300]{0,1:T(8,128)} %bitcast.2) | data formatting | bytes 614400

commit v7 on v6

--- a/solution.py
+++ b/solution.py
@@ -248,7 +248,7 @@
             g_copy(c, 2 * p).start()
             g_copy(c, 2 * p + 1).start()
 
-            @pl.when(r == FIRST)
+            @pl.when(jnp.logical_or(r == FIRST, jnp.logical_not(chain)))
             def _():
                 g_copy(c, 2 * p).wait_send()
                 g_copy(c, 2 * p + 1).wait_send()
@@ -501,7 +501,7 @@
 
     @pl.loop(0, CHUNKS)
     def _(i):
-        @pl.when(jnp.logical_and(gives, r != FIRST))
+        @pl.when(jnp.logical_and(gives, chain))
         def _():
             g_copy(c, i).wait_send()
 

time: 122 us -> 122 us (level)
  no operation moved by 1% of the time
where the time goes in v7:
time: 122 us; the launch traced here: 121 us
  Pallas kernels  118 us (97%)
  local copies, waits for them, and re-layouts  3.25 us (3%)
    pallas_call x1, Pallas kernels, body(): pl.pallas_call(kernel, out_shape=(jax.ShapeDtypeStruct((DATES, PIECE), F3...  118 us
    unnamed x2, local copies, waits for them, and re-layouts  3.25 us

profile of v7, /device:TPU:45, one launch (start us, length us, event | category | flops | bytes accessed | tf_op | source)
XLA Modules:
  0.0 121.4 jit_solution(13860944051389856874)
XLA Ops:
  0.6 117.6 %shard_map.68 = (f32[300,256]{1,0:T(8,128)}, f32[64,300]{1,0:T(8,128)}) custom-call(s32[8]{0:T(128)} %step_ref.1, s32[16,128]{1,0:T(8,128)} %bitcast.3, f32[300,256]{1,0:T(8,128)} %ser_ref.1, f32[2048,1024]{1,0:T(8,128)} %panel_ref.1, f32[2048,1024]{1,0:T(8,128)} %diag_ref.1), custom_call_target="tpu_custom_call" | custom-call | tf_op jit(solution)/shard_map/pallas_call | solution.py:545
  118.2 1.5 %copy.9 = f32[64,300]{1,0:T(8,128)} copy(f32[64,300]{1,0:T(8,128)} %get-tuple-element.8) | data formatting | bytes 153600
  119.7 1.7 %copy.10 = f32[256,300]{0,1:T(8,128)} copy(f32[256,300]{0,1:T(8,128)} %bitcast.2) | data formatting | bytes 614400
